TPU v7x, 128 devices: a whole 4x4x4 slice. The times are simulated.
128 devices in a mesh: row: 16 (over y, x), col: 2 (over core), rep: 4 (over z).
Axes of the slice: x: 4, y: 4, z: 4, core: 2. Of those that a mesh axis runs over, the one named last changes fastest.
Arguments:
- amplitudes: bfloat16 [16, 16, 768, 768], P(None, 'rep', ('row', 'col')), may hold values from -6 to 6
- integrals: bfloat16 [16, 768, 16, 768], P('rep', 'row', 'col'), may hold values from -0.0546875 to 0.0546875
- pair_mask: int32 [16, 16], P(None, 'rep'), may hold values 0 or 1
- tile_mask: int32 [16, 6, 16, 6], P('rep', None, 'col'), may hold values 0 or 1
Outputs:
- cycle: float32 [16, 16, 768, 768], P('row', 'col', 'rep')
All inputs are finite; a program needn't handle non-finite values. No bound on the sum of `pair_mask` or of `tile_mask` on one device may be relied on, other than what follows from the above.
Results may differ from a plain program's by a relative error of at most 0.0003.
Values may be sent and summed in bfloat16 or wider, within the bound.
A program may use at most 192 MiB of HBM per device.

v0:
```python
import jax
import jax.numpy as jnp
from jax import lax
from jax.sharding import PartitionSpec as P

TILE = 128


def on_device(amplitudes, integrals, pair_mask, tile_mask):
    kept = amplitudes * pair_mask[:, :, None, None].astype(jnp.bfloat16)
    krows, cwidth, jcols, bwidth = integrals.shape
    ntiles = tile_mask.shape[1]
    cglobal = lax.axis_index("row") * cwidth + jnp.arange(cwidth, dtype=jnp.int32)
    onehot = (cglobal[:, None] // TILE == jnp.arange(ntiles, dtype=jnp.int32)[None, :]).astype(
        jnp.float32
    )
    rowmask = jnp.einsum("ktjs,ct->kcjs", tile_mask.astype(jnp.float32), onehot)
    fullmask = jnp.repeat(rowmask, TILE, axis=3)
    sparse = integrals * fullmask.astype(jnp.bfloat16)
    wide = lax.all_gather(kept, "col", axis=2, tiled=True)
    left = lax.all_to_all(wide, "row", split_axis=0, concat_axis=2, tiled=True)
    total = jnp.einsum(
        "ikac,kcjb->aijb",
        left,
        lax.all_gather(sparse, "row", axis=1, tiled=True),
        preferred_element_type=jnp.float32,
    )
    share = lax.psum_scatter(total, "rep", scatter_dimension=0, tiled=True)
    return share.transpose(1, 2, 0, 3)


def solution(mesh):
    placed = (
        P(None, "rep", ("row", "col"), None),
        P("rep", "row", "col", None),
        P(None, "rep"),
        P("rep", None, "col", None),
    )
    return jax.shard_map(
        on_device,
        mesh=mesh,
        in_specs=placed,
        out_specs=P("row", "col", "rep", None),
        check_vma=False,
    )
```

profile of v0, /device:TPU:8, one launch (start us, length us, event | category | flops | bytes accessed | tf_op | source)
XLA Modules:
  0.0 526.1 jit_solution(8241602372288946661)
XLA Ops:
  6.5 0.0 copy-start.1
  6.5 0.0 all-gather.5.cloned.1.call-start
  6.5 0.7 convert_element_type.22
  7.3 0.1 copy.22
  7.4 0.0 copy-start
  7.4 3.4 broadcast_multiply_fusion
  10.8 0.0 all-gather.5.cloned.1.call-update
  10.8 0.0 all-gather.3.cloned.1.call-start
  10.9 0.0 copy-done.1
  10.9 0.2 fusion
  11.1 0.3 copy.19
  11.4 1.5 broadcast_bitcast_fusion
  12.9 0.0 copy-done
  12.9 2.8 copy_multiply_fusion
  15.7 0.0 all-gather.3.cloned.1.call-update
  15.7 0.0 reduce-scatter.2.cloned.1.call-start
  15.8 14.7 %all-gather.5.cloned.1.call-done = bf16[16,4,48,768]{3,2,1,0:T(8,128)(2,1)} async-done(((bf16[16,4,24,768]{3,2,1,0:T(8,128)(2,1)}), bf16[16,4,48,768]{3,2,1,0:T(8,128)(2,1)}) %all-gather.5.cloned.1.call-update) | async-done | bytes 4718608 | tf_op jit(solution)/shard_map/all_gather | solution.py:20
  30.5 99.5 %all_to_all.15 = bf16[16,4,48,768]{3,2,1,0:T(8,128)(2,1)S(1)} all-to-all(bf16[16,4,48,768]{3,2,1,0:T(8,128)(2,1)} %all-gather.5.cloned.1.call-done), channel_id=1, replica_groups=mesh['row'=16,'col'=2,'rep'=4] {'row'}, dimensions={0} | all-to-all | bytes 9437184 | tf_op jit(solution)/shard_map/all_to_all | solution.py:21
  130.0 2.5 copy.23
  132.6 160.3 %all-gather.3.cloned.1.call-done = bf16[4,768,8,768]{3,1,0,2:T(8,128)(2,1)} async-done(((bf16[4,48,8,768]{3,1,0,2:T(8,128)(2,1)}), bf16[4,768,8,768]{3,1,0,2:T(8,128)(2,1)}) %all-gather.3.cloned.1.call-update) | async-done | bytes 37748752 | tf_op jit(solution)/shard_map/all_gather | solution.py:25
  292.9 36.4 %convolution_bitcast_fusion = f32[768,1,8,768]{0,3,2,1:T(8,128)} fusion(bf16[4,768,8,768]{3,1,0,2:T(8,128)(2,1)} %all-gather.3.cloned.1.call-done, bf16[4,768,768,1]{2,1,0,3:T(8,128)(2,1)} %bitcast.26), kind=kOutput, calls=%fused_computation | convolution fusion | flops 28991029248 | bytes 61341696 | tf_op jit(solution)/shard_map/ikac,kcjb->aijb/dot_general | solution.py:22
  329.3 19.2 %copy.24 = f32[768,1,8,768]{3,2,1,0:T(8,128)} copy(f32[768,1,8,768]{0,3,2,1:T(8,128)} %convolution_bitcast_fusion) | data formatting | bytes 37748736 | tf_op jit(solution)/shard_map/ikac,kcjb->aijb/transpose | solution.py:22
  348.6 0.0 reduce-scatter.2.cloned.1.call-update
  348.6 165.0 %reduce-scatter.2.cloned.1.call-done = f32[192,1,8,768]{3,2,1,0:T(8,128)} async-done(((f32[768,1,8,768]{3,2,1,0:T(8,128)}), f32[192,1,8,768]{3,2,1,0:T(8,128)}) %reduce-scatter.2.cloned.1.call-update) | async-done | bytes 4718608 | tf_op jit(solution)/shard_map/reduce_scatter | solution.py:28
  513.6 6.0 %copy.25 = f32[1,8,192,768]{3,2,1,0:T(8,128)} copy(f32[1,8,192,768]{3,1,0,2:T(8,128)} %bitcast.25) | data formatting | bytes 9437184 | tf_op jit(solution)/shard_map/transpose | solution.py:29
  (2 shorter events, 0.0 us)
Async XLA Ops:
  6.5 4.3 copy-start.1
  6.5 24.0 %all-gather.5.cloned.1.call-start = ((), (), s32[]{:S(2)}) async-start(), calls=%async_computation.3 | async-start | bytes 7077888 | tf_op jit(solution)/shard_map/all_gather | solution.py:20
  7.4 5.5 %copy-start = (bf16[4,48,8,768]{3,2,1,0:T(8,128)(2,1)S(1)}, bf16[4,48,8,768]{3,2,1,0:T(8,128)(2,1)}, u32[]{:S(2)}) copy-start(bf16[4,48,8,768]{3,2,1,0:T(8,128)(2,1)} %param.5) | copy-start | bytes 7077892
  10.8 282.1 %all-gather.3.cloned.1.call-start = ((), (), s32[]{:S(2)}) async-start(), calls=%async_computation.2 | async-start | bytes 40108032 | tf_op jit(solution)/shard_map/all_gather | solution.py:25
  15.7 497.8 %reduce-scatter.2.cloned.1.call-start = ((), (), s32[]{:S(2)}) async-start(), calls=%async_computation.4 | async-start | bytes 23592960 | tf_op jit(solution)/shard_map/reduce_scatter | solution.py:28
Sparse Core Ops, SparseCore 0:
  10.9 19.4 all-gather.4
  32.6 260.2 all-gather.2
  348.7 164.8 reduce-scatter.1
where the time goes:
time: 528 us; the launch traced here: 526 us
  waiting for transfers between devices  340 us (64%)
  blocking collectives  99.5 us (19%)
  matrix products  36.6 us (7%)
  local copies, waits for them, and re-layouts  29.7 us (6%)
  between operations  13.2 us (2%)
  other arithmetic  6.99 us (1%)
    reduce_scatter x1, waiting for transfers between devices, on_device(): share = lax.psum_scatter(total, 'rep', scatter_dimension=0, tiled=True)  165 us
    all_gather x1, waiting for transfers between devices, on_device(): lax.all_gather(sparse, 'row', axis=1, tiled=True)  160 us
    all_to_all x1, blocking collectives, on_device(): left = lax.all_to_all(wide, 'row', split_axis=0, concat_axis=2, tiled=True)  99.5 us
    dot_general x1, matrix products, on_device(): jnp.einsum('ikac,kcjb->aijb', left, lax.all_gather(sparse, 'row', axis=1,...  36.4 us
    transpose x1, local copies, waits for them, and re-layouts, on_device(): jnp.einsum('ikac,kcjb->aijb', left, lax.all_gather(sparse, 'row', axis=1,...  19.2 us
    all_gather x1, waiting for transfers between devices, on_device(): wide = lax.all_gather(kept, 'col', axis=2, tiled=True)  14.7 us
  transfers between devices with their start and end apart: 3, of which 3 were waited for; matrix products, arithmetic and copies ran while one was open for 1% of the time, Pallas kernels for 0%

commit v1 on v0

v1 whole, which is shorter than its diff:
```python
import jax
import jax.numpy as jnp
from jax import lax
from jax.experimental import pallas as pl
from jax.experimental.pallas import tpu as pltpu
from jax.sharding import PartitionSpec as P

TILE = 128
MESH = pl.DeviceIdType.MESH
NS = 6
NB = 256
QROWS = 192
SROWS = 208
TOP = 32766.0


def quantised(value):
    top = jnp.maximum(jnp.max(jnp.abs(value), axis=0, keepdims=True), 1e-30)
    power = jnp.ceil(jnp.log2(top))
    coded = jnp.round(value * (jnp.exp2(-power) * TOP)).astype(jnp.int16)
    return coded, jnp.broadcast_to(power, (16, NB)).astype(jnp.int16)


def restored(ref):
    power = ref[QROWS:SROWS, :].astype(jnp.float32)[0:1]
    return ref[0:QROWS, :].astype(jnp.float32) * (jnp.exp2(power) * (1.0 / TOP))


def kernel(
    ls, rs, out, lbuf, rbuf, own, tot, zs, zr, xs, xr_,
    la_s, la_r, ld_s, ld_r, lr_s, lr_r, dd_s, dd_r,
    ra_s, ra_r, rd_s, rd_r, rr_s, rr_r, z_s, z_r, x_s, x_r,
):
    row, core, z = lax.axis_index("row"), lax.axis_index("col"), lax.axis_index("rep")
    y, x = row // 4, row % 4

    def at_x(d):
        return (y * 4 + (x + d) % 4, core, z)

    def at_y(d):
        return ((y + d) % 4 * 4 + x, core, z)

    def at_z(d):
        return (row, core, (z + d) % 4)

    partner = (row, 1 - core, z)
    everyone = [f(d) for f in (at_x, at_y, at_z) for d in (1, 2, 3)] + [partner]

    def remote(src, dst, send, recv, device):
        return pltpu.make_async_remote_copy(
            src_ref=src, dst_ref=dst, send_sem=send, recv_sem=recv, device_id=device, device_id_type=MESH
        )

    def arrived(ref, sem):
        pltpu.make_async_copy(ref, ref, sem).wait()

    def off_of(q):
        return jnp.where(q == 0, 2, jnp.where(q == 1, 1, jnp.where(q == 2, 3, 0)))

    def y_of(q):
        return (z + off_of(q)) % 4

    def lpiece(yy, xx, first=0, rows=96, side=None):
        side = core if side is None else side
        return lbuf.at[yy * 4 + xx, pl.ds(pl.multiple_of(side * 96 + first, 16), rows)]

    def la_copy(d):
        return remote(ls.at[(y + d) % 4], lpiece(y, x), la_s.at[d - 1], la_r.at[4 - d], at_y(d))

    def la_local():
        return pltpu.make_async_copy(ls.at[y], lpiece(y, x), la_r.at[0])

    def ld_copy(q, way):
        ref = lpiece(y_of(q), x)
        return remote(ref, ref, ld_s.at[q, way], ld_r.at[q, way], at_x(1 if way == 0 else 3))

    def lr_copy(q, way):
        ref = lpiece(y_of(q), (x + (3 if way == 0 else 1)) % 4, 48 * way, 48)
        return remote(ref, ref, lr_s.at[q, way], lr_r.at[q, way], at_x(1 if way == 0 else 3))

    def dd_copy(q, xr):
        ref = lpiece(y_of(q), (x + xr) % 4)
        return remote(ref, ref, dd_s.at[q, xr], dd_r.at[q, xr], partner)

    def rpiece(s, xx):
        return rbuf.at[s, :, pl.ds(pl.multiple_of((y * 4 + xx) * 48, 16), 48), :]

    def rblock(s, yy, k0=0, nk=4):
        return rbuf.at[s, pl.ds(k0, nk), pl.ds(pl.multiple_of(yy * 192, 16), 192), :]

    def ra_copy(s, d):
        return remote(rs.at[(x + d) % 4, s], rpiece(s, x), ra_s.at[s, d - 1], ra_r.at[s, 4 - d], at_x(d))

    def ra_local(s):
        return pltpu.make_async_copy(rs.at[x, s], rpiece(s, x), ra_r.at[s, 0])

    def rd_copy(s, way):
        ref = rblock(s, y)
        return remote(ref, ref, rd_s.at[s, way], rd_r.at[s, way], at_y(1 if way == 0 else 3))

    def rr_copy(s, way):
        ref = rblock(s, (y + (3 if way == 0 else 1)) % 4, 2 * way, 2)
        return remote(ref, ref, rr_s.at[s, way], rr_r.at[s, way], at_y(1 if way == 0 else 3))

    def z_copy(q, xr, s):
        return remote(zs.at[q, xr, s], zr.at[q, xr, s], z_s.at[q, xr, s], z_r.at[q, xr, s], at_z(off_of(q)))

    def x_copy(s, d):
        return remote(xs.at[s, d - 1], xr_.at[s, d - 1], x_s.at[s, d - 1], x_r.at[s, d - 1], at_x(d))

    def ra_start(s):
        for d in (1, 3, 2):
            ra_copy(s, d).start()

    def rd_start(s):
        for d in range(4):
            arrived(rpiece(s, (x + d) % 4), ra_r.at[s, d])
        for way in (0, 1):
            rd_copy(s, way).start()

    def rr_start(s):
        for way in (0, 1):
            arrived(rblock(s, (y + (3 if way == 0 else 1)) % 4), rd_r.at[s, way])
            rr_copy(s, way).start()

    def rr_wait(s):
        for way in (0, 1):
            arrived(rblock(s, (y + 2) % 4, 2 * way, 2), rr_r.at[s, way])

    def ld_start(q):
        for way in (0, 1):
            ld_copy(q, way).start()

    def lr_start(q):
        for way in (0, 1):
            xr = 3 if way == 0 else 1
            arrived(lpiece(y_of(q), (x + xr) % 4), ld_r.at[q, way])
            lr_copy(q, way).start()
            dd_copy(q, xr).start()

    def lr_done(q):
        for way in (0, 1):
            arrived(lpiece(y_of(q), (x + 2) % 4, 48 * way, 48), lr_r.at[q, way])
        dd_copy(q, 2).start()

    def dd_wait(q, xr):
        arrived(lpiece(y_of(q), (x + xr) % 4, side=1 - core), dd_r.at[q, xr])

    def product(q, xr, s):
        src = y_of(q) * 4 + (x + xr) % 4
        value = jnp.dot(lbuf[src], rbuf[s].reshape(3072, NB), preferred_element_type=jnp.float32)

        @pl.when(q == 3)
        def _():
            own[s, xr] = value

        @pl.when(q < 3)
        def _():
            coded, power = quantised(value)
            zs[q, xr, s, 0:QROWS, :] = coded
            zs[q, xr, s, QROWS:SROWS, :] = power
            z_copy(q, xr, s).start()

    barrier = pltpu.get_barrier_semaphore()
    for device in everyone:
        pl.semaphore_signal(barrier, inc=1, device_id=device, device_id_type=MESH)
    pl.semaphore_wait(barrier, len(everyone))

    ra_start(0)
    for d in (1, 3, 2):
        la_copy(d).start()
    la_local().start()
    for s in range(NS):
        ra_local(s).start()
    ra_start(1)
    ra_start(2)
    rd_start(0)
    rd_start(1)

    def own_column(q, carry):
        yy = y_of(q)
        arrived(lpiece(yy, x), la_r.at[(yy - y + 4) % 4])

        @pl.when(q < 2)
        def _():
            ld_start(q)

        dd_copy(q, 0).start()
        return carry

    lax.fori_loop(0, 4, own_column, 0)
    rr_start(0)

    def step(s, carry):
        @pl.when(s < NS - 3)
        def _():
            ra_start(s + 3)

        @pl.when(s < NS - 2)
        def _():
            rd_start(s + 2)

        @pl.when(s < NS - 1)
        def _():
            rr_start(s + 1)

        @pl.when(s < 4)
        def _():
            lr_start(s)

        @pl.when((s >= 1) & (s < 3))
        def _():
            ld_start(s + 1)

        @pl.when((s >= 1) & (s < 5))
        def _():
            lr_done(s - 1)

        rr_wait(s)

        @pl.when(s == 0)
        def _():
            for q in range(4):
                dd_wait(q, 0)

        before = 4 + 3 * jnp.maximum(s - 1, 0)
        fresh = jnp.where((s >= 1) & (s < 5), 3 * (s + 1), 0)

        def one(n, carry):
            m = n - before
            late = n >= before
            first = n < 4
            q = jnp.where(late, s - 1, jnp.where(first, n, (n - 4) // 3))
            xr = jnp.where(late, 1 + m % 3, jnp.where(first, 0, 1 + (n - 4) % 3))
            part = jnp.where(late, m // 3, s)

            @pl.when(late & (m < 3))
            def _():
                dd_wait(q, xr)

            product(q, xr, part)
            return carry

        lax.fori_loop(0, before + fresh, one, 0)
        return carry

    lax.fori_loop(0, NS, step, 0)

    def reduce(s):
        jj, bt = s // 3, s % 3

        def gather(xr, carry):
            total = own[s, xr]
            for q in range(3):
                arrived(zr.at[q, xr, s], z_r.at[q, xr, s])
                total = total + restored(zr.at[q, xr, s])
            tot[(x + xr) % 4] = total
            return carry

        lax.fori_loop(0, 4, gather, 0)

        def rows_of(i):
            return jnp.concatenate(
                [
                    tot[xx, pl.ds(pl.multiple_of(side * 96 + i * 24, 8), 24), :]
                    for xx in range(4)
                    for side in range(2)
                ],
                axis=0,
            )

        def give(d, carry):
            coded, power = quantised(rows_of((x + d) % 4))
            xs[s, d - 1, 0:QROWS, :] = coded
            xs[s, d - 1, QROWS:SROWS, :] = power
            x_copy(s, d).start()
            return carry

        lax.fori_loop(1, 4, give, 0)
        out[0, x * 2 + jj, :, pl.ds(pl.multiple_of(bt * NB, NB), NB)] = rows_of(x)

    def finish(s):
        jj, bt = s // 3, s % 3

        def take(d, carry):
            arrived(xr_.at[s, d - 1], x_r.at[s, d - 1])
            xx = (x - d + 4) % 4
            out[0, xx * 2 + jj, :, pl.ds(pl.multiple_of(bt * NB, NB), NB)] = restored(xr_.at[s, d - 1])
            return carry

        lax.fori_loop(1, 4, take, 0)

    def tail(s, carry):
        @pl.when(s < NS)
        def _():
            reduce(s)

        @pl.when(s >= 1)
        def _():
            finish(s - 1)

        return carry

    lax.fori_loop(0, NS + 1, tail, 0)

    for d in (1, 2, 3):
        la_copy(d).wait_send()

    def sent_right(s, carry):
        for d in (1, 2, 3):
            ra_copy(s, d).wait_send()
            x_copy(s, d).wait_send()
        for way in (0, 1):
            rd_copy(s, way).wait_send()
            rr_copy(s, way).wait_send()
        return carry

    def sent_left(q, carry):
        for way in (0, 1):
            ld_copy(q, way).wait_send()
            lr_copy(q, way).wait_send()
        for xr in range(4):
            dd_copy(q, xr).wait_send()
        return carry

    def sent_z(n, carry):
        z_copy(n // 24, n // 6 % 4, n % 6).wait_send()
        return carry

    lax.fori_loop(0, NS, sent_right, 0)
    lax.fori_loop(0, 4, sent_left, 0)
    lax.fori_loop(0, 72, sent_z, 0)


def on_device(amplitudes, integrals, pair_mask, tile_mask):
    kept = amplitudes * pair_mask[:, :, None, None].astype(jnp.bfloat16)
    ls = kept.transpose(0, 2, 1, 3).reshape(4, 96, 3072)
    krows, cwidth, jcols, bwidth = integrals.shape
    ntiles = tile_mask.shape[1]
    cglobal = lax.axis_index("row") * cwidth + jnp.arange(cwidth, dtype=jnp.int32)
    onehot = (cglobal[:, None] // TILE == jnp.arange(ntiles, dtype=jnp.int32)[None, :]).astype(jnp.float32)
    rowmask = jnp.einsum("ktjs,ct->kcjs", tile_mask.astype(jnp.float32), onehot)
    fullmask = jnp.repeat(rowmask, TILE, axis=3)
    sparse = integrals * fullmask.astype(jnp.bfloat16)
    rs = sparse.reshape(krows, cwidth, 4, 2, 3, NB).transpose(2, 3, 4, 0, 1, 5).reshape(4, NS, krows, cwidth, NB)
    dma = pltpu.SemaphoreType.DMA
    bf, i16, f32 = jnp.bfloat16, jnp.int16, jnp.float32
    return pl.pallas_call(
        kernel,
        out_shape=jax.ShapeDtypeStruct((1, 8, QROWS, 768), f32),
        in_specs=[pl.BlockSpec(memory_space=pl.ANY)] * 2,
        out_specs=pl.BlockSpec(memory_space=pltpu.VMEM),
        scratch_shapes=[
            pltpu.VMEM((16, 192, 3072), bf),
            pltpu.VMEM((NS, 4, 768, NB), bf),
            pltpu.VMEM((NS, 4, QROWS, NB), f32),
            pltpu.VMEM((4, QROWS, NB), f32),
            pltpu.VMEM((3, 4, NS, SROWS, NB), i16),
            pltpu.VMEM((3, 4, NS, SROWS, NB), i16),
            pltpu.VMEM((NS, 3, SROWS, NB), i16),
            pltpu.VMEM((NS, 3, SROWS, NB), i16),
            dma((3,)), dma((4,)), dma((4, 2)), dma((4, 2)), dma((4, 2)), dma((4, 2)), dma((4, 4)), dma((4, 4)),
            dma((NS, 3)), dma((NS, 4)), dma((NS, 2)), dma((NS, 2)), dma((NS, 2)), dma((NS, 2)),
            dma((3, 4, NS)), dma((3, 4, NS)), dma((NS, 3)), dma((NS, 3)),
        ],
        compiler_params=pltpu.CompilerParams(
            collective_id=0, has_side_effects=True, vmem_limit_bytes=63 * 2**20
        ),
        cost_estimate=pl.CostEstimate(flops=29 * 10**9, bytes_accessed=10**7, transcendentals=0),
    )(ls, rs)


def solution(mesh):
    placed = (
        P(None, "rep", ("row", "col"), None),
        P("rep", "row", "col", None),
        P(None, "rep"),
        P("rep", None, "col", None),
    )
    return jax.shard_map(
        on_device,
        mesh=mesh,
        in_specs=placed,
        out_specs=P("row", "col", "rep", None),
        check_vma=False,
    )
```

time: 528 us -> 227 us (0.43)
  waiting for transfers between devices: 340 us -> 0 us
  Pallas kernels: 0 us -> 204 us
  blocking collectives: 99.5 us -> 0 us
  matrix products: 36.6 us -> 0.2 us
  between operations: 13.2 us -> 0.06 us
  local copies, waits for them, and re-layouts: 29.7 us -> 17 us
    pallas_call x0 -> x1, Pallas kernels: none -> 204 us  [on_device(): pl.pallas_call(kernel, out_shape=jax.ShapeDtypeStruct((1, 8, QROWS, 768),...]
    all_gather x2 -> x0, waiting for transfers between devices: 175 us -> none  [the longest x1 160 us: on_device(): lax.all_gather(sparse, 'row', axis=1, tiled=True)]
    reduce_scatter x1 -> x0, waiting for transfers between devices: 165 us -> none  [on_device(): share = lax.psum_scatter(total, 'rep', scatter_dimension=0, tiled=True)]
    all_to_all x1 -> x0, blocking collectives: 99.5 us -> none  [on_device(): left = lax.all_to_all(wide, 'row', split_axis=0, concat_axis=2, tiled=True)]
    dot_general x1 -> x0, matrix products: 36.4 us -> none  [on_device(): jnp.einsum('ikac,kcjb->aijb', left, lax.all_gather(sparse, 'row', axis=1,...]
    transpose x2, local copies, waits for them, and re-layouts: 25.3 us -> 4.27 us  [the longest x1 3.17 us: on_device(): sparse.reshape(krows, cwidth, 4, 2, 3, NB).transpose(2, 3, 4, 0, 1, 5)]
    reshape x0 -> x2, local copies, waits for them, and re-layouts: none -> 7.49 us  [the longest x1 4.55 us: on_device(): sparse.reshape(krows, cwidth, 4, 2, 3, NB).transpose(2, 3, 4, 0, 1, 5)]
  transfers between devices with their start and end apart: 3 -> 0, of which waited for: 3 -> 0; matrix products, arithmetic and copies ran while one was open for 1% -> 0% of each run, Pallas kernels for 0% -> 0%
where the time goes in v1:
time: 227 us
  Pallas kernels  204 us (90%)
  local copies, waits for them, and re-layouts  17 us (7%)
  other arithmetic  5.47 us (2%)
    pallas_call x1, Pallas kernels, on_device(): pl.pallas_call(kernel, out_shape=jax.ShapeDtypeStruct((1, 8, QROWS, 768),...  204 us
    unnamed x3, local copies, waits for them, and re-layouts  4.83 us
    reshape x1, local copies, waits for them, and re-layouts, on_device(): sparse.reshape(krows, cwidth, 4, 2, 3, NB).transpose(2, 3, 4, 0, 1, 5)  4.55 us

profile of v1, /device:TPU:8, one launch (start us, length us, event | category | flops | bytes accessed | tf_op | source)
XLA Modules:
  0.0 227.1 jit_solution(6378681331585259912)
XLA Ops:
  0.0 0.7 convert_element_type.18
  0.7 0.1 copy.10
  0.8 0.9 convert_element_type.19
  1.7 0.2 fusion
  1.9 0.3 copy.13
  2.2 3.7 %bitcast_multiply_fusion = bf16[4,48,8,768]{3,2,1,0:T(8,128)(2,1)} fusion(bf16[4,48,8,768]{3,2,1,0:T(8,128)(2,1)} %param.5, bf16[4,48,8,6]{2,3,1,0:T(8,128)(2,1)S(1)} %copy.13), kind=kLoop, calls=%fused_computation | loop fusion | flops 1179648 | bytes 4737024 | tf_op jit(solution)/shard_map/mul | solution.py:344
  5.8 4.6 %reshape.51 = bf16[4,48,4,2,3,256]{5,4,3,2,1,0:T(4,128)(2,1)S(1)} reshape(bf16[4,48,8,768]{3,2,1,0:T(8,128)(2,1)} %bitcast_multiply_fusion) | data formatting | bytes 4718592 | tf_op jit(solution)/shard_map/reshape | solution.py:345
  10.4 0.0 copy-start
  10.4 3.2 %copy.14 = bf16[4,2,3,4,48,256]{5,4,3,2,1,0:T(8,128)(2,1)} copy(bf16[4,2,3,4,48,256]{5,2,1,0,4,3:T(4,128)(2,1)S(1)} %bitcast.15) | data formatting | bytes 4718592 | tf_op jit(solution)/shard_map/transpose | solution.py:345
  13.6 0.0 copy-done
  13.6 0.2 multiply_bitcast_fusion
  13.8 1.1 copy.11
  14.9 2.9 %reshape.50.ls = bf16[4,96,3072]{2,1,0:T(8,128)(2,1)} reshape(bf16[16,24,4,768]{3,2,1,0:T(4,128)(2,1)S(1)} %copy.11) | data formatting | bytes 4718592 | tf_op jit(solution)/shard_map/reshape | solution.py:337
  17.8 204.4 %shard_map.46 = f32[1,8,192,768]{3,2,1,0:T(8,128)} custom-call(bf16[4,96,3072]{2,1,0:T(8,128)(2,1)} %reshape.50.ls, bf16[4,6,4,48,256]{4,3,2,1,0:T(8,128)(2,1)} %bitcast.16), custom_call_target="tpu_custom_call" | custom-call | flops 28999999488 | bytes 10000000 | tf_op jit(solution)/shard_map/pallas_call | solution.py:348
  222.2 4.8 %copy.19 = f32[1,8,192,768]{3,2,1,0:T(8,128)} copy(f32[1,8,192,768]{3,2,1,0:T(8,128)} %shard_map.46) | data formatting | bytes 9437184
  (1 shorter events, 0.0 us)
Async XLA Ops:
  10.4 3.2 %copy-start = (bf16[16,4,24,768]{3,2,1,0:T(8,128)(2,1)S(1)}, bf16[16,4,24,768]{3,2,1,0:T(8,128)(2,1)}, u32[]{:S(2)}) copy-start(bf16[16,4,24,768]{3,2,1,0:T(8,128)(2,1)} %param.4) | copy-start | bytes 7077892

commit v2 on v0

v2 whole, which is shorter than its diff:
```python
import jax
import jax.numpy as jnp
from jax import lax
from jax.experimental import pallas as pl
from jax.experimental.pallas import tpu as pltpu
from jax.sharding import PartitionSpec as P

TILE = 128
MESH = pl.DeviceIdType.MESH
NS = 6
NB = 256
QROWS = 192
SROWS = 208
HROWS = 96
HS = 112
PARTS = ((0, 1, 3), (2,))
TOP = 32766.0


EVENTS = (
    (0, "ra", 0), (0, "ra", 1), (0, "ra", 2), (0, "LA", 0), (0, "ld", 0), (0, "ra", 3), (0, "la", 1),
    (0, "la", 3), (0, "RA", 0), (0, "rd", 0), (0, "la", 2), (0, "RA", 1), (0, "LA", 1), (0, "LA", 2),
    (0, "ld", 2), (0, "ld", 1), (0, "RD", 0), (0, "LD", 0), (0, "rr", 0), (0, "rd", 1), (0, "RA", 2),
    (0, "rd", 2), (0, "RA", 3), (0, "LA", 3), (0, "ld", 3), (0, "ra", 4), (0, "RR", 0), (0, "DD", (0, 0)),
    (1, "DD", (1, 0)), (2, "DD", (2, 0)), (3, "DD", (3, 0)), (4, "DD", (0, 1)), (5, "LD", 2), (5, "lr", 2),
    (5, "ra", 5), (5, "lr", 0), (5, "RD", 1), (5, "rr", 1), (5, "DD", (2, 1)), (6, "RD", 2), (6, "LD", 1),
    (6, "rr", 2), (6, "rd", 3), (6, "RR", 1), (10, "DD", (1, 1)), (12, "RR", 2), (18, "LD", 3), (18, "lr", 3),
    (18, "lr", 1), (21, "RA", 4), (21, "RD", 3), (21, "rr", 3), (21, "rd", 4), (21, "DD", (3, 1)),
    (24, "RR", 3), (25, "LR", 2), (31, "RA", 5), (31, "rd", 5), (32, "DD", (2, 2)), (36, "RD", 4),
    (36, "rr", 4), (36, "LR", 0), (36, "DD", (0, 2)), (40, "RD", 5), (40, "rr", 5), (40, "LR", 3),
    (40, "DD", (3, 2)), (42, "RR", 4), (47, "LR", 1), (48, "RR", 5), (58, "DD", (1, 2)),
)
BLOCKS = (
    (0, 0, 0), (1, 0, 0), (2, 0, 0), (3, 0, 0), (0, 1, 0), (2, 1, 0), (0, 0, 1), (1, 0, 1), (2, 0, 1),
    (3, 0, 1), (1, 1, 0), (0, 1, 1), (0, 0, 2), (1, 0, 2), (2, 0, 2), (3, 0, 2), (1, 1, 1), (2, 1, 1),
    (0, 1, 2), (1, 1, 2), (2, 1, 2), (3, 1, 0), (3, 1, 1), (3, 1, 2), (0, 0, 3), (1, 0, 3), (2, 0, 3),
    (3, 0, 3), (0, 1, 3), (1, 1, 3), (2, 1, 3), (3, 1, 3), (2, 2, 0), (2, 2, 1), (2, 2, 2), (2, 2, 3),
    (0, 2, 0), (0, 2, 1), (0, 2, 2), (0, 2, 3), (3, 2, 0), (3, 2, 1), (0, 0, 4), (1, 0, 4), (2, 0, 4),
    (3, 0, 4), (0, 1, 4), (1, 1, 4), (0, 0, 5), (1, 0, 5), (2, 0, 5), (3, 0, 5), (2, 1, 4), (3, 1, 4),
    (0, 1, 5), (1, 1, 5), (2, 1, 5), (3, 1, 5), (1, 2, 0), (1, 2, 1), (1, 2, 2), (3, 2, 2), (1, 2, 3),
    (3, 2, 3), (0, 2, 4), (1, 2, 4), (2, 2, 4), (3, 2, 4), (0, 2, 5), (1, 2, 5), (2, 2, 5), (3, 2, 5),
)
LAG = 10
SUMS = ((47, 47, 47, 49, 71, 75), (76, 77, 79, 81, 81, 81))
ROUNDS = 82


def quantised(value):
    top = jnp.maximum(jnp.max(jnp.abs(value), axis=0, keepdims=True), 1e-30)
    power = jnp.ceil(jnp.log2(top))
    coded = jnp.round(value * (jnp.exp2(-power) * TOP)).astype(jnp.int16)
    return coded, jnp.broadcast_to(power, (16, NB)).astype(jnp.int16)


def restored(ref, rows=QROWS):
    power = ref[rows : rows + 16, :].astype(jnp.float32)[0:1]
    return ref[0:rows, :].astype(jnp.float32) * (jnp.exp2(power) * (1.0 / TOP))


def kernel(
    ls, rs, out, lbuf, rbuf, own, tot, val, hs, hr, zs, zr, xs0, xr0, xs1, xr1,
    la_s, la_r, ld_s, ld_r, lr_s, lr_r, dd_s, dd_r,
    ra_s, ra_r, rd_s, rd_r, rr_s, rr_r, h_s, h_r, z_s, z_r, x0_s, x0_r, x1_s, x1_r,
):
    row, core, z = lax.axis_index("row"), lax.axis_index("col"), lax.axis_index("rep")
    y, x = row // 4, row % 4

    def at_x(d):
        return (y * 4 + (x + d) % 4, core, z)

    def at_y(d):
        return ((y + d) % 4 * 4 + x, core, z)

    def at_z(d):
        return (row, core, (z + d) % 4)

    partner = (row, 1 - core, z)
    everyone = [f(d) for f in (at_x, at_y, at_z) for d in (1, 2, 3)] + [partner]

    def remote(src, dst, send, recv, device):
        return pltpu.make_async_remote_copy(
            src_ref=src, dst_ref=dst, send_sem=send, recv_sem=recv, device_id=device, device_id_type=MESH
        )

    def arrived(ref, sem):
        pltpu.make_async_copy(ref, ref, sem).wait()

    def rel_of(p):
        return jnp.where(p < 2, p, 5 - p)

    def y_at(p):
        return (y + rel_of(p)) % 4

    def lpiece(yy, xx, first=0, rows=96, side=None):
        side = core if side is None else side
        return lbuf.at[yy * 4 + xx, :, pl.ds(pl.multiple_of(side * 96 + first, 16), rows), :]

    def la_copy(d):
        return remote(ls.at[(y + d) % 4], lpiece(y, x), la_s.at[d - 1], la_r.at[4 - d], at_y(d))

    def la_local():
        return pltpu.make_async_copy(ls.at[y], lpiece(y, x), la_r.at[0])

    def ld_copy(p, way):
        ref = lpiece(y_at(p), x)
        return remote(ref, ref, ld_s.at[p, way], ld_r.at[p, way], at_x(1 if way == 0 else 3))

    def lr_copy(p, way):
        ref = lpiece(y_at(p), (x + (3 if way == 0 else 1)) % 4, 48 * way, 48)
        return remote(ref, ref, lr_s.at[p, way], lr_r.at[p, way], at_x(1 if way == 0 else 3))

    def dd_copy(p, xr):
        ref = lpiece(y_at(p), (x + xr) % 4)
        return remote(ref, ref, dd_s.at[p, xr], dd_r.at[p, xr], partner)

    def rpiece(s, xx):
        return rbuf.at[s, :, pl.ds(pl.multiple_of((y * 4 + xx) * 48, 16), 48), :]

    def rblock(s, yy, k0=0, nk=4):
        return rbuf.at[s, pl.ds(k0, nk), pl.ds(pl.multiple_of(yy * 192, 16), 192), :]

    def ra_copy(s, d):
        return remote(rs.at[(x + d) % 4, s], rpiece(s, x), ra_s.at[s, d - 1], ra_r.at[s, 4 - d], at_x(d))

    def ra_local(s):
        return pltpu.make_async_copy(rs.at[x, s], rpiece(s, x), ra_r.at[s, 0])

    def rd_copy(s, way):
        ref = rblock(s, y)
        return remote(ref, ref, rd_s.at[s, way], rd_r.at[s, way], at_y(1 if way == 0 else 3))

    def rr_copy(s, way):
        ref = rblock(s, (y + (3 if way == 0 else 1)) % 4, 2 * way, 2)
        return remote(ref, ref, rr_s.at[s, way], rr_r.at[s, way], at_y(1 if way == 0 else 3))

    def h_copy(xr, s, way):
        return remote(
            hs.at[xr, s, way], hr.at[xr, s, way], h_s.at[xr, s, way], h_r.at[xr, s, way], at_z(1 if way == 0 else 3)
        )

    def z_copy(way, xr, s):
        return remote(
            zs.at[way, xr, s], zr.at[way, xr, s], z_s.at[way, xr, s], z_r.at[way, xr, s], at_z(1 + 2 * way)
        )

    def x0_copy(s, d):
        return remote(xs0.at[s, d - 1], xr0.at[s, d - 1], x0_s.at[s, d - 1], x0_r.at[s, d - 1], at_x(d))

    def x1_copy(s, d):
        return remote(xs1.at[s, d - 1], xr1.at[s, d - 1], x1_s.at[s, d - 1], x1_r.at[s, d - 1], at_x(d))

    def ra_start(s):
        for d in (1, 3, 2):
            ra_copy(s, d).start()

    def ra_wait(s):
        for d in range(4):
            arrived(rpiece(s, (x + d) % 4), ra_r.at[s, d])

    def rd_start(s):
        for way in (0, 1):
            rd_copy(s, way).start()

    def rd_wait(s):
        for way in (0, 1):
            arrived(rblock(s, (y + (3 if way == 0 else 1)) % 4), rd_r.at[s, way])

    def rr_start(s):
        for way in (0, 1):
            rr_copy(s, way).start()

    def rr_wait(s):
        for way in (0, 1):
            arrived(rblock(s, (y + 2) % 4, 2 * way, 2), rr_r.at[s, way])

    def la_wait(p):
        d = rel_of(p)
        arrived(lpiece(y_at(p), x), la_r.at[d])
        dd_copy(p, 0).start()

    def ld_start(p):
        for way in (0, 1):
            ld_copy(p, way).start()

    def ld_wait(p):
        for way in (0, 1):
            xr = 3 if way == 0 else 1
            arrived(lpiece(y_at(p), (x + xr) % 4), ld_r.at[p, way])
            dd_copy(p, xr).start()

    def lr_start(p):
        for way in (0, 1):
            lr_copy(p, way).start()

    def lr_done(p):
        for way in (0, 1):
            arrived(lpiece(y_at(p), (x + 2) % 4, 48 * way, 48), lr_r.at[p, way])
        dd_copy(p, 2).start()

    def dd_wait(p, xr):
        arrived(lpiece(y_at(p), (x + xr) % 4, side=1 - core), dd_r.at[p, xr])

    def product(p, pieces, s):
        left = jnp.concatenate(
            [
                jnp.concatenate([lbuf[y_at(p) * 4 + (x + xr) % 4, k] for k in range(4)], axis=1)
                for xr in pieces
            ],
            axis=0,
        )
        return jnp.dot(left, rbuf[s].reshape(3072, NB), preferred_element_type=jnp.float32)

    def give_on(value, off, xr, s):
        @pl.when(off == 0)
        def _():
            own[s, xr] = value

        @pl.when(off == 2)
        def _():
            for way in (0, 1):
                coded, power = quantised(value[HROWS * way : HROWS * (way + 1)])
                hs[xr, s, way, 0:HROWS, :] = coded
                hs[xr, s, way, HROWS:HS, :] = power
                h_copy(xr, s, way).start()

        for way in (0, 1):

            @pl.when(off == 1 + 2 * way)
            def _(way=way):
                arrived(hr.at[xr, s, way], h_r.at[xr, s, way])
                more = restored(hr.at[xr, s, way], HROWS)
                first, second = value[0:HROWS], value[HROWS:QROWS]
                if way == 0:
                    first = first + more
                else:
                    second = second + more
                coded, power = quantised(jnp.concatenate([first, second], axis=0))
                zs[way, xr, s, 0:QROWS, :] = coded
                zs[way, xr, s, QROWS:SROWS, :] = power
                z_copy(way, xr, s).start()

    barrier = pltpu.get_barrier_semaphore()
    for device in everyone:
        pl.semaphore_signal(barrier, inc=1, device_id=device, device_id_type=MESH)
    pl.semaphore_wait(barrier, len(everyone))

    la_local().start()
    for s in range(NS):
        ra_local(s).start()

    does = {
        "ra": ra_start, "rd": rd_start, "rr": rr_start, "ld": ld_start, "lr": lr_start,
        "la": lambda d: la_copy(d).start(),
        "RA": ra_wait, "RD": rd_wait, "RR": rr_wait, "LA": la_wait, "LD": ld_wait, "LR": lr_done,
        "DD": lambda k: [dd_wait(k[0], xr) for xr in ((0,), (1, 3), (2,))[k[1]]],
    }

    def look(i):
        codes = [p * 32 + kind * 8 + s for p, kind, s in BLOCKS]
        word = 0
        for n in range(0, len(codes), 4):
            word = jnp.where(i // 4 == n // 4, sum(c * 128**m for m, c in enumerate(codes[n : n + 4])), word)
        m = i % 4
        shift = jnp.where(m == 0, 1, jnp.where(m == 1, 128, jnp.where(m == 2, 128**2, 128**3)))
        code = word // shift % 128
        return (i >= 0) & (i < len(codes)), code // 32, code // 8 % 4, code % 8

    def reduce(s, part):
        jj, bt = s // 3, s % 3
        pieces = PARTS[part]
        rows = 48 * len(pieces)
        sent, begin = (xs0, x0_copy) if part == 0 else (xs1, x1_copy)
        for xr in pieces:
            total = own[s, xr]
            for way in (0, 1):
                arrived(zr.at[way, xr, s], z_r.at[way, xr, s])
                total = total + restored(zr.at[way, xr, s])
            tot[xr] = total

        def rows_of(i):
            return [
                tot[xr, pl.ds(pl.multiple_of(side * 96 + i * 24, 8), 24), :] for xr in pieces for side in range(2)
            ]

        def give(d, carry):
            coded, power = quantised(jnp.concatenate(rows_of((x + d) % 4), axis=0))
            sent[s, d - 1, 0:rows, :] = coded
            sent[s, d - 1, rows : rows + 16, :] = power
            begin(s, d).start()
            return carry

        lax.fori_loop(1, 4, give, 0)
        place(s, part, x, jnp.concatenate(rows_of(x), axis=0))

    def place(s, part, source, value):
        jj, bt = s // 3, s % 3
        for n, xr in enumerate(PARTS[part]):
            at = pl.multiple_of((source + xr) % 4 * 48, 8)
            out[0, source * 2 + jj, pl.ds(at, 48), pl.ds(pl.multiple_of(bt * NB, NB), NB)] = value[48 * n : 48 * n + 48]

    def round_(i, carry):
        for n in range(len(BLOCKS) + 1):
            todo = [(what, k) for m, what, k in EVENTS if m == n]
            if todo:

                @pl.when(i == n)
                def _(todo=todo):
                    for what, k in todo:
                        does[what](k)

        def half(j, carry):
            there, p, kind, s = look(i - LAG * j)
            off = (y_at(p) - z + 4) % 4

            @pl.when(there & (off % 2 == j))
            def _():
                @pl.when(kind == 1)
                def _():
                    val[...] = product(p, (1, 3), s).reshape(2, QROWS, NB)

                @pl.when(kind != 1)
                def _():
                    val[0] = product(p, (kind,), s)

                def one(n, carry):
                    give_on(val[n], off, jnp.where(kind == 1, 1 + 2 * n, kind), s)
                    return carry

                lax.fori_loop(0, jnp.where(kind == 1, 2, 1), one, 0)

            return carry

        lax.fori_loop(0, 2, half, 0)

        for part in range(2):

            def sums(s, carry, part=part):
                reduce(s, part)
                return carry

            begun = sum(jnp.where(i > n, 1, 0) for n in SUMS[part])
            lax.fori_loop(begun, sum(jnp.where(i >= n, 1, 0) for n in SUMS[part]), sums, 0)
        return carry

    lax.fori_loop(0, ROUNDS, round_, 0)

    def finish(s, carry):
        def take(d, carry):
            arrived(xr0.at[s, d - 1], x0_r.at[s, d - 1])
            place(s, 0, (x - d + 4) % 4, restored(xr0.at[s, d - 1], 144))
            arrived(xr1.at[s, d - 1], x1_r.at[s, d - 1])
            place(s, 1, (x - d + 4) % 4, restored(xr1.at[s, d - 1], 48))
            return carry

        return lax.fori_loop(1, 4, take, carry)

    lax.fori_loop(0, NS, finish, 0)

    for d in (1, 2, 3):
        la_copy(d).wait_send()

    def sent_right(s, carry):
        for d in (1, 2, 3):
            ra_copy(s, d).wait_send()
            x0_copy(s, d).wait_send()
            x1_copy(s, d).wait_send()
        for way in (0, 1):
            rd_copy(s, way).wait_send()
            rr_copy(s, way).wait_send()
        return carry

    def sent_left(q, carry):
        for way in (0, 1):
            ld_copy(q, way).wait_send()
            lr_copy(q, way).wait_send()
        for xr in range(4):
            dd_copy(q, xr).wait_send()
        return carry

    def sent_z(n, carry):
        for way in (0, 1):
            h_copy(n // 6, n % 6, way).wait_send()
            z_copy(way, n // 6, n % 6).wait_send()
        return carry

    lax.fori_loop(0, NS, sent_right, 0)
    lax.fori_loop(0, 4, sent_left, 0)
    lax.fori_loop(0, 24, sent_z, 0)


def right_kernel(mask, w, rs):
    k = pl.program_id(0)
    first = lax.axis_index("row") * 48
    tile = first // TILE
    after = jnp.minimum(tile + 1, 5)
    edge = (tile + 1) * TILE - first
    upper = lax.broadcasted_iota(jnp.int32, (48, TILE), 0) < edge
    rows = jnp.swapaxes(w[0].astype(jnp.float32), 0, 1)
    for j in range(8):
        for b in range(6):
            kept = jnp.where(upper, mask[k, tile, j, b].astype(jnp.float32), mask[k, after, j, b].astype(jnp.float32))
            rs[j // 2, j % 2 * 3 + b // 2, 0, :, b % 2 * TILE : (b % 2 + 1) * TILE] = (
                rows[j, :, b * TILE : (b + 1) * TILE] * kept
            ).astype(jnp.bfloat16)


def on_device(amplitudes, integrals, pair_mask, tile_mask):
    kept = amplitudes * pair_mask[:, :, None, None].astype(jnp.bfloat16)
    ls = kept.reshape(4, 4, 4, 24, 768).transpose(0, 2, 1, 3, 4).reshape(4, 4, 96, 768)
    rs = pl.pallas_call(
        right_kernel,
        grid=(4,),
        out_shape=jax.ShapeDtypeStruct((4, NS, 4, 48, NB), jnp.bfloat16),
        in_specs=[
            pl.BlockSpec(memory_space=pltpu.SMEM),
            pl.BlockSpec((1, 48, 8, 768), lambda k: (k, 0, 0, 0)),
        ],
        out_specs=pl.BlockSpec((4, NS, 1, 48, NB), lambda k: (0, 0, k, 0, 0)),
        cost_estimate=pl.CostEstimate(flops=10**6, bytes_accessed=5 * 10**6, transcendentals=0),
    )(tile_mask, integrals)
    dma = pltpu.SemaphoreType.DMA
    bf, i16, f32 = jnp.bfloat16, jnp.int16, jnp.float32
    return pl.pallas_call(
        kernel,
        out_shape=jax.ShapeDtypeStruct((1, 8, QROWS, 768), f32),
        in_specs=[pl.BlockSpec(memory_space=pl.ANY)] * 2,
        out_specs=pl.BlockSpec(memory_space=pltpu.VMEM),
        scratch_shapes=[
            pltpu.VMEM((16, 4, 192, 768), bf),
            pltpu.VMEM((NS, 4, 768, NB), bf),
            pltpu.VMEM((NS, 4, QROWS, NB), f32),
            pltpu.VMEM((4, QROWS, NB), f32),
            pltpu.VMEM((2, QROWS, NB), f32),
            pltpu.VMEM((4, NS, 2, HS, NB), i16),
            pltpu.VMEM((4, NS, 2, HS, NB), i16),
            pltpu.VMEM((2, 4, NS, SROWS, NB), i16),
            pltpu.VMEM((2, 4, NS, SROWS, NB), i16),
            pltpu.VMEM((NS, 3, 160, NB), i16),
            pltpu.VMEM((NS, 3, 160, NB), i16),
            pltpu.VMEM((NS, 3, 64, NB), i16),
            pltpu.VMEM((NS, 3, 64, NB), i16),
            dma((3,)), dma((4,)), dma((4, 2)), dma((4, 2)), dma((4, 2)), dma((4, 2)), dma((4, 4)), dma((4, 4)),
            dma((NS, 3)), dma((NS, 4)), dma((NS, 2)), dma((NS, 2)), dma((NS, 2)), dma((NS, 2)),
            dma((4, NS, 2)), dma((4, NS, 2)), dma((2, 4, NS)), dma((2, 4, NS)), dma((NS, 3)), dma((NS, 3)),
            dma((NS, 3)), dma((NS, 3)),
        ],
        compiler_params=pltpu.CompilerParams(
            collective_id=0, has_side_effects=True, vmem_limit_bytes=63 * 2**20
        ),
        cost_estimate=pl.CostEstimate(flops=29 * 10**9, bytes_accessed=10**7, transcendentals=0),
    )(ls, rs)


def solution(mesh):
    placed = (
        P(None, "rep", ("row", "col"), None),
        P("rep", "row", "col", None),
        P(None, "rep"),
        P("rep", None, "col", None),
    )
    return jax.shard_map(
        on_device,
        mesh=mesh,
        in_specs=placed,
        out_specs=P("row", "col", "rep", None),
        check_vma=False,
    )
```

time: 528 us -> 195 us (0.37)
  waiting for transfers between devices: 340 us -> 0 us
  Pallas kernels: 0 us -> 183 us
  blocking collectives: 99.5 us -> 0 us
  matrix products: 36.6 us -> 0 us
  local copies, waits for them, and re-layouts: 29.7 us -> 8.33 us
  between operations: 13.2 us -> 0.02 us
  other arithmetic: 6.99 us -> 0.9 us
    pallas_call x0 -> x2, Pallas kernels: none -> 183 us  [the longest x1 177 us: on_device(): pl.pallas_call(kernel, out_shape=jax.ShapeDtypeStruct((1, 8, QROWS, 768),...]
    all_gather x2 -> x0, waiting for transfers between devices: 175 us -> none  [the longest x1 160 us: on_device(): lax.all_gather(sparse, 'row', axis=1, tiled=True)]
    reduce_scatter x1 -> x0, waiting for transfers between devices: 165 us -> none  [on_device(): share = lax.psum_scatter(total, 'rep', scatter_dimension=0, tiled=True)]
    all_to_all x1 -> x0, blocking collectives: 99.5 us -> none  [on_device(): left = lax.all_to_all(wide, 'row', split_axis=0, concat_axis=2, tiled=True)]
    dot_general x2 -> x0, matrix products: 36.6 us -> none  [the longest x1 36.4 us: on_device(): jnp.einsum('ikac,kcjb->aijb', left, lax.all_gather(sparse, 'row', axis=1,...]
    transpose x2 -> x0, local copies, waits for them, and re-layouts: 25.3 us -> none  [the longest x1 19.2 us: on_device(): jnp.einsum('ikac,kcjb->aijb', left, lax.all_gather(sparse, 'row', axis=1,...]
    unnamed x4, local copies, waits for them, and re-layouts: 0.01 us -> 6.56 us
  transfers between devices with their start and end apart: 3 -> 0, of which waited for: 3 -> 0; matrix products, arithmetic and copies ran while one was open for 1% -> 0% of each run, Pallas kernels for 0% -> 0%
where the time goes in v2:
time: 195 us; the launch traced here: 192 us
  Pallas kernels  183 us (94%)
  local copies, waits for them, and re-layouts  8.33 us (4%)
    pallas_call x1, Pallas kernels, on_device(): pl.pallas_call(kernel, out_shape=jax.ShapeDtypeStruct((1, 8, QROWS, 768),...  177 us
    unnamed x4, local copies, waits for them, and re-layouts  6.56 us
    pallas_call x1, Pallas kernels, on_device(): pl.pallas_call(right_kernel, grid=(4,), out_shape=jax.ShapeDtypeStruct((4...  6.14 us

profile of v2, /device:TPU:8, one launch (start us, length us, event | category | flops | bytes accessed | tf_op | source)
XLA Modules:
  0.0 192.1 jit_solution(11303238929848912833)
XLA Ops:
  0.0 0.7 convert_element_type.4
  0.7 0.1 copy.5
  0.8 1.7 copy.7.mask
  2.5 0.0 copy-start
  2.5 6.1 %shard_map.46.rs = bf16[4,6,4,48,256]{4,3,2,1,0:T(8,128)(2,1)} custom-call(s32[4,6,8,6]{3,2,1,0:T(8,128)} %copy.7.mask, bf16[4,48,8,768]{3,2,1,0:T(8,128)(2,1)} %w.1), custom_call_target="tpu_custom_call" | custom-call | flops 1000000 | bytes 5000000 | tf_op jit(solution)/shard_map/pallas_call | solution.py:410
  8.7 0.0 copy-done
  8.7 0.2 broadcast_multiply_fusion
  8.9 1.7 copy.6
  10.6 176.7 %shard_map.47 = f32[1,8,192,768]{3,2,1,0:T(8,128)} custom-call(bf16[4,4,96,768]{3,2,1,0:T(8,128)(2,1)} %bitcast.5, bf16[4,6,4,48,256]{4,3,2,1,0:T(8,128)(2,1)} %shard_map.46.rs), custom_call_target="tpu_custom_call" | custom-call | flops 28999999488 | bytes 10000000 | tf_op jit(solution)/shard_map/pallas_call | solution.py:423
  187.3 4.8 %copy.9 = f32[1,8,192,768]{3,2,1,0:T(8,128)} copy(f32[1,8,192,768]{3,2,1,0:T(8,128)} %shard_map.47) | data formatting | bytes 9437184
Async XLA Ops:
  2.5 6.1 %copy-start = (bf16[16,4,24,768]{3,2,1,0:T(8,128)(2,1)S(1)}, bf16[16,4,24,768]{3,2,1,0:T(8,128)(2,1)}, u32[]{:S(2)}) copy-start(bf16[16,4,24,768]{3,2,1,0:T(8,128)(2,1)} %param.4) | copy-start | bytes 7077892

commit v3 on v2

--- a/solution.py
+++ b/solution.py
@@ -10,9 +10,13 @@
 NS = 6
 NB = 256
 QROWS = 192
-SROWS = 208
 HROWS = 96
-HS = 112
+
+
+def coded_shape(rows):
+    return (2 * rows + 16, 128)
+
+
 PARTS = ((0, 1, 3), (2,))
 TOP = 32766.0
 
@@ -45,20 +49,28 @@
 ROUNDS = 82
 
 
-def quantised(value):
+def write_coded(ref, value):
+    rows = value.shape[0]
     top = jnp.maximum(jnp.max(jnp.abs(value), axis=0, keepdims=True), 1e-30)
     power = jnp.ceil(jnp.log2(top))
     coded = jnp.round(value * (jnp.exp2(-power) * TOP)).astype(jnp.int16)
-    return coded, jnp.broadcast_to(power, (16, NB)).astype(jnp.int16)
-
-
-def restored(ref, rows=QROWS):
-    power = ref[rows : rows + 16, :].astype(jnp.float32)[0:1]
-    return ref[0:rows, :].astype(jnp.float32) * (jnp.exp2(power) * (1.0 / TOP))
+    ref[0:rows, :] = coded[:, 0:128]
+    ref[rows : 2 * rows, :] = coded[:, 128:256]
+    first = lax.broadcasted_iota(jnp.int32, (16, 128), 0) < 8
+    ref[2 * rows : 2 * rows + 16, :] = jnp.where(first, power[:, 0:128], power[:, 128:256]).astype(jnp.int16)
+
+
+def restored(ref, rows):
+    power = ref[2 * rows : 2 * rows + 16, :].astype(jnp.float32)
+    scale = jnp.exp2(power) * (1.0 / TOP)
+    return jnp.concatenate(
+        [ref[0:rows, :].astype(jnp.float32) * scale[0:1], ref[rows : 2 * rows, :].astype(jnp.float32) * scale[8:9]],
+        axis=1,
+    )
 
 
 def kernel(
-    ls, rs, out, lbuf, rbuf, own, tot, val, hs, hr, zs, zr, xs0, xr0, xs1, xr1,
+    ls, rs, kept, xr0, xr1, lbuf, rbuf, own, tot, val, hs, hr, zs, zr, xs0, xs1,
     la_s, la_r, ld_s, ld_r, lr_s, lr_r, dd_s, dd_r,
     ra_s, ra_r, rd_s, rd_r, rr_s, rr_r, h_s, h_r, z_s, z_r, x0_s, x0_r, x1_s, x1_r,
 ):
@@ -218,9 +230,7 @@
         @pl.when(off == 2)
         def _():
             for way in (0, 1):
-                coded, power = quantised(value[HROWS * way : HROWS * (way + 1)])
-                hs[xr, s, way, 0:HROWS, :] = coded
-                hs[xr, s, way, HROWS:HS, :] = power
+                write_coded(hs.at[xr, s, way], value[HROWS * way : HROWS * (way + 1)])
                 h_copy(xr, s, way).start()
 
         for way in (0, 1):
@@ -234,9 +244,7 @@
                     first = first + more
                 else:
                     second = second + more
-                coded, power = quantised(jnp.concatenate([first, second], axis=0))
-                zs[way, xr, s, 0:QROWS, :] = coded
-                zs[way, xr, s, QROWS:SROWS, :] = power
+                write_coded(zs.at[way, xr, s], jnp.concatenate([first, second], axis=0))
                 z_copy(way, xr, s).start()
 
     barrier = pltpu.get_barrier_semaphore()
@@ -266,15 +274,13 @@
         return (i >= 0) & (i < len(codes)), code // 32, code // 8 % 4, code % 8
 
     def reduce(s, part):
-        jj, bt = s // 3, s % 3
         pieces = PARTS[part]
-        rows = 48 * len(pieces)
         sent, begin = (xs0, x0_copy) if part == 0 else (xs1, x1_copy)
         for xr in pieces:
             total = own[s, xr]
             for way in (0, 1):
                 arrived(zr.at[way, xr, s], z_r.at[way, xr, s])
-                total = total + restored(zr.at[way, xr, s])
+                total = total + restored(zr.at[way, xr, s], QROWS)
             tot[xr] = total
 
         def rows_of(i):
@@ -283,30 +289,32 @@
             ]
 
         def give(d, carry):
-            coded, power = quantised(jnp.concatenate(rows_of((x + d) % 4), axis=0))
-            sent[s, d - 1, 0:rows, :] = coded
-            sent[s, d - 1, rows : rows + 16, :] = power
+            write_coded(sent.at[s, d - 1], jnp.concatenate(rows_of((x + d) % 4), axis=0))
             begin(s, d).start()
             return carry
 
         lax.fori_loop(1, 4, give, 0)
-        place(s, part, x, jnp.concatenate(rows_of(x), axis=0))
-
-    def place(s, part, source, value):
-        jj, bt = s // 3, s % 3
-        for n, xr in enumerate(PARTS[part]):
-            at = pl.multiple_of((source + xr) % 4 * 48, 8)
-            out[0, source * 2 + jj, pl.ds(at, 48), pl.ds(pl.multiple_of(bt * NB, NB), NB)] = value[48 * n : 48 * n + 48]
+        own_rows = rows_of(x)
+        for n, xr in enumerate(pieces):
+            kept[s, xr] = jnp.concatenate(own_rows[2 * n : 2 * n + 2], axis=0)
 
     def round_(i, carry):
-        for n in range(len(BLOCKS) + 1):
+        def events(n):
             todo = [(what, k) for m, what, k in EVENTS if m == n]
             if todo:
 
                 @pl.when(i == n)
-                def _(todo=todo):
+                def _():
                     for what, k in todo:
                         does[what](k)
+
+        for g in range(0, len(BLOCKS), 9):
+            if any(g <= m < g + 9 for m, _, _ in EVENTS):
+
+                @pl.when((i >= g) & (i < g + 9))
+                def _(g=g):
+                    for n in range(g, g + 9):
+                        events(n)
 
         def half(j, carry):
             there, p, kind, s = look(i - LAG * j)
@@ -344,26 +352,12 @@
 
     lax.fori_loop(0, ROUNDS, round_, 0)
 
-    def finish(s, carry):
-        def take(d, carry):
-            arrived(xr0.at[s, d - 1], x0_r.at[s, d - 1])
-            place(s, 0, (x - d + 4) % 4, restored(xr0.at[s, d - 1], 144))
-            arrived(xr1.at[s, d - 1], x1_r.at[s, d - 1])
-            place(s, 1, (x - d + 4) % 4, restored(xr1.at[s, d - 1], 48))
-            return carry
-
-        return lax.fori_loop(1, 4, take, carry)
-
-    lax.fori_loop(0, NS, finish, 0)
-
     for d in (1, 2, 3):
         la_copy(d).wait_send()
 
     def sent_right(s, carry):
         for d in (1, 2, 3):
             ra_copy(s, d).wait_send()
-            x0_copy(s, d).wait_send()
-            x1_copy(s, d).wait_send()
         for way in (0, 1):
             rd_copy(s, way).wait_send()
             rr_copy(s, way).wait_send()
@@ -386,6 +380,29 @@
     lax.fori_loop(0, NS, sent_right, 0)
     lax.fori_loop(0, 4, sent_left, 0)
     lax.fori_loop(0, 24, sent_z, 0)
+
+    def finish(s, carry):
+        for d in (1, 2, 3):
+            arrived(xr0.at[s, d - 1], x0_r.at[s, d - 1])
+            arrived(xr1.at[s, d - 1], x1_r.at[s, d - 1])
+            x0_copy(s, d).wait_send()
+            x1_copy(s, d).wait_send()
+        return carry
+
+    lax.fori_loop(0, NS, finish, 0)
+
+
+def place_kernel(kept, came0, came1, out):
+    x = lax.axis_index("row") % 4
+    for bt in range(3):
+        for d in range(4):
+            source = (x - d + 4) % 4
+            if d:
+                first, last = restored(came0.at[bt, d - 1], 144), restored(came1.at[bt, d - 1], 48)
+            for n, xr in enumerate((0, 1, 3, 2)):
+                value = kept[bt, xr] if d == 0 else last if xr == 2 else first[48 * n : 48 * n + 48]
+                at = pl.multiple_of((source + xr) % 4 * 48, 8)
+                out[0, source, 0, pl.ds(at, 48), bt * NB : bt * NB + NB] = value
 
 
 def right_kernel(mask, w, rs):
@@ -395,13 +412,13 @@
     after = jnp.minimum(tile + 1, 5)
     edge = (tile + 1) * TILE - first
     upper = lax.broadcasted_iota(jnp.int32, (48, TILE), 0) < edge
-    rows = jnp.swapaxes(w[0].astype(jnp.float32), 0, 1)
+    rows = jnp.swapaxes(w[0], 0, 1)
     for j in range(8):
         for b in range(6):
             kept = jnp.where(upper, mask[k, tile, j, b].astype(jnp.float32), mask[k, after, j, b].astype(jnp.float32))
             rs[j // 2, j % 2 * 3 + b // 2, 0, :, b % 2 * TILE : (b % 2 + 1) * TILE] = (
-                rows[j, :, b * TILE : (b + 1) * TILE] * kept
-            ).astype(jnp.bfloat16)
+                rows[j, :, b * TILE : (b + 1) * TILE] * kept.astype(jnp.bfloat16)
+            )
 
 
 def on_device(amplitudes, integrals, pair_mask, tile_mask):
@@ -420,25 +437,28 @@
     )(tile_mask, integrals)
     dma = pltpu.SemaphoreType.DMA
     bf, i16, f32 = jnp.bfloat16, jnp.int16, jnp.float32
-    return pl.pallas_call(
+    came = ((NS, 3) + coded_shape(144), (NS, 3) + coded_shape(48))
+    parts = pl.pallas_call(
         kernel,
-        out_shape=jax.ShapeDtypeStruct((1, 8, QROWS, 768), f32),
+        out_shape=(
+            jax.ShapeDtypeStruct((NS, 4, 48, NB), f32),
+            jax.ShapeDtypeStruct(came[0], i16),
+            jax.ShapeDtypeStruct(came[1], i16),
+        ),
         in_specs=[pl.BlockSpec(memory_space=pl.ANY)] * 2,
-        out_specs=pl.BlockSpec(memory_space=pltpu.VMEM),
+        out_specs=[pl.BlockSpec(memory_space=pltpu.VMEM)] * 3,
         scratch_shapes=[
             pltpu.VMEM((16, 4, 192, 768), bf),
             pltpu.VMEM((NS, 4, 768, NB), bf),
             pltpu.VMEM((NS, 4, QROWS, NB), f32),
             pltpu.VMEM((4, QROWS, NB), f32),
             pltpu.VMEM((2, QROWS, NB), f32),
-            pltpu.VMEM((4, NS, 2, HS, NB), i16),
-            pltpu.VMEM((4, NS, 2, HS, NB), i16),
-            pltpu.VMEM((2, 4, NS, SROWS, NB), i16),
-            pltpu.VMEM((2, 4, NS, SROWS, NB), i16),
-            pltpu.VMEM((NS, 3, 160, NB), i16),
-            pltpu.VMEM((NS, 3, 160, NB), i16),
-            pltpu.VMEM((NS, 3, 64, NB), i16),
-            pltpu.VMEM((NS, 3, 64, NB), i16),
+            pltpu.VMEM((4, NS, 2) + coded_shape(HROWS), i16),
+            pltpu.VMEM((4, NS, 2) + coded_shape(HROWS), i16),
+            pltpu.VMEM((2, 4, NS) + coded_shape(QROWS), i16),
+            pltpu.VMEM((2, 4, NS) + coded_shape(QROWS), i16),
+            pltpu.VMEM((NS, 3) + coded_shape(144), i16),
+            pltpu.VMEM((NS, 3) + coded_shape(48), i16),
             dma((3,)), dma((4,)), dma((4, 2)), dma((4, 2)), dma((4, 2)), dma((4, 2)), dma((4, 4)), dma((4, 4)),
             dma((NS, 3)), dma((NS, 4)), dma((NS, 2)), dma((NS, 2)), dma((NS, 2)), dma((NS, 2)),
             dma((4, NS, 2)), dma((4, NS, 2)), dma((2, 4, NS)), dma((2, 4, NS)), dma((NS, 3)), dma((NS, 3)),
@@ -449,6 +469,19 @@
         ),
         cost_estimate=pl.CostEstimate(flops=29 * 10**9, bytes_accessed=10**7, transcendentals=0),
     )(ls, rs)
+    done = pl.pallas_call(
+        place_kernel,
+        grid=(2,),
+        out_shape=jax.ShapeDtypeStruct((1, 4, 2, QROWS, 768), f32),
+        in_specs=[
+            pl.BlockSpec((3, 4, 48, NB), lambda s: (s, 0, 0, 0)),
+            pl.BlockSpec((3,) + came[0][1:], lambda s: (s, 0, 0, 0)),
+            pl.BlockSpec((3,) + came[1][1:], lambda s: (s, 0, 0, 0)),
+        ],
+        out_specs=pl.BlockSpec((1, 4, 1, QROWS, 768), lambda s: (0, 0, s, 0, 0)),
+        cost_estimate=pl.CostEstimate(flops=10**7, bytes_accessed=8 * 10**6, transcendentals=0),
+    )(*parts)
+    return done.reshape(1, 8, QROWS, 768)
 
 
 def solution(mesh):

time: 195 us -> 187 us (0.959)
  local copies, waits for them, and re-layouts: 8.33 us -> 3.51 us
  Pallas kernels: 183 us -> 180 us
    unnamed x4 -> x3, local copies, waits for them, and re-layouts: 6.56 us -> 1.74 us
    pallas_call x1 -> x2, Pallas kernels: 177 us -> 174 us  [the longest x1 170 us: on_device(): pl.pallas_call(kernel, out_shape=(jax.ShapeDtypeStruct((NS, 4, 48, NB), f...]
where the time goes in v3:
time: 187 us; the launch traced here: 184 us
  Pallas kernels  180 us (96%)
  local copies, waits for them, and re-layouts  3.51 us (2%)
    pallas_call x1, Pallas kernels, on_device(): pl.pallas_call(kernel, out_shape=(jax.ShapeDtypeStruct((NS, 4, 48, NB), f...  170 us
    pallas_call x1, Pallas kernels, on_device(): pl.pallas_call(right_kernel, grid=(4,), out_shape=jax.ShapeDtypeStruct((4...  5.88 us
    pallas_call x1, Pallas kernels, on_device(): pl.pallas_call(place_kernel, grid=(2,), out_shape=jax.ShapeDtypeStruct((1...  3.83 us

profile of v3, /device:TPU:8, one launch (start us, length us, event | category | flops | bytes accessed | tf_op | source)
XLA Modules:
  0.0 184.2 jit_solution(18275811621194727668)
XLA Ops:
  0.0 0.7 convert_element_type.4
  0.7 0.1 copy.5
  0.8 1.7 copy.7.mask
  2.5 0.0 copy-start
  2.5 5.9 %shard_map.46.rs = bf16[4,6,4,48,256]{4,3,2,1,0:T(8,128)(2,1)} custom-call(s32[4,6,8,6]{3,2,1,0:T(8,128)} %copy.7.mask, bf16[4,48,8,768]{3,2,1,0:T(8,128)(2,1)} %w.1), custom_call_target="tpu_custom_call" | custom-call | flops 1000000 | bytes 5000000 | tf_op jit(solution)/shard_map/pallas_call | solution.py:427
  8.4 0.0 copy-done
  8.4 0.2 broadcast_multiply_fusion
  8.6 1.7 copy.6
  10.3 170.1 %shard_map.47 = (f32[6,4,48,256]{3,2,1,0:T(8,128)}, s16[6,3,304,128]{3,2,1,0:T(8,128)(2,1)}, s16[6,3,112,128]{3,2,1,0:T(8,128)(2,1)}) custom-call(bf16[4,4,96,768]{3,2,1,0:T(8,128)(2,1)} %bitcast.6, bf16[4,6,4,48,256]{4,3,2,1,0:T(8,128)(2,1)} %shard_map.46.rs), custom_call_target="tpu_custom_call" | custom-call | flops 28999999488 | bytes 10000000 | tf_op jit(solution)/shard_map/pallas_call | solution.py:441
  180.4 3.8 %shard_map.48 = f32[1,4,2,192,768]{4,3,2,1,0:T(8,128)} custom-call(f32[6,4,48,256]{3,2,1,0:T(8,128)} %get-tuple-element.8.kept, s16[6,3,304,128]{3,2,1,0:T(8,128)(2,1)} %get-tuple-element.9.came0, s16[6,3,112,128]{3,2,1,0:T(8,128)(2,1)} %get-tuple-element.10.came1), custom_call_target="tpu_custom_call" | custom-call | flops 10000000 | bytes 8000000 | tf_op jit(solution)/shard_map/pallas_call | solution.py:472
Async XLA Ops:
  2.5 5.9 %copy-start = (bf16[16,4,24,768]{3,2,1,0:T(8,128)(2,1)S(1)}, bf16[16,4,24,768]{3,2,1,0:T(8,128)(2,1)}, u32[]{:S(2)}) copy-start(bf16[16,4,24,768]{3,2,1,0:T(8,128)(2,1)} %param.4) | copy-start | bytes 7077892

commit v4 on v3

--- a/solution.py
+++ b/solution.py
@@ -19,41 +19,43 @@
 
 PARTS = ((0, 1, 3), (2,))
 TOP = 32766.0
+ROUND = 12582912.0
 
 
 EVENTS = (
-    (0, "ra", 0), (0, "ra", 1), (0, "ra", 2), (0, "LA", 0), (0, "ld", 0), (0, "ra", 3), (0, "la", 1),
-    (0, "la", 3), (0, "RA", 0), (0, "rd", 0), (0, "la", 2), (0, "RA", 1), (0, "LA", 1), (0, "LA", 2),
-    (0, "ld", 2), (0, "ld", 1), (0, "RD", 0), (0, "LD", 0), (0, "rr", 0), (0, "rd", 1), (0, "RA", 2),
-    (0, "rd", 2), (0, "RA", 3), (0, "LA", 3), (0, "ld", 3), (0, "ra", 4), (0, "RR", 0), (0, "DD", (0, 0)),
-    (1, "DD", (1, 0)), (2, "DD", (2, 0)), (3, "DD", (3, 0)), (4, "DD", (0, 1)), (5, "LD", 2), (5, "lr", 2),
-    (5, "ra", 5), (5, "lr", 0), (5, "RD", 1), (5, "rr", 1), (5, "DD", (2, 1)), (6, "RD", 2), (6, "LD", 1),
-    (6, "rr", 2), (6, "rd", 3), (6, "RR", 1), (10, "DD", (1, 1)), (12, "RR", 2), (18, "LD", 3), (18, "lr", 3),
-    (18, "lr", 1), (21, "RA", 4), (21, "RD", 3), (21, "rr", 3), (21, "rd", 4), (21, "DD", (3, 1)),
-    (24, "RR", 3), (25, "LR", 2), (31, "RA", 5), (31, "rd", 5), (32, "DD", (2, 2)), (36, "RD", 4),
-    (36, "rr", 4), (36, "LR", 0), (36, "DD", (0, 2)), (40, "RD", 5), (40, "rr", 5), (40, "LR", 3),
-    (40, "DD", (3, 2)), (42, "RR", 4), (47, "LR", 1), (48, "RR", 5), (58, "DD", (1, 2)),
+    (0, "ra", 0), (0, "ra", 1), (0, "ra", 2), (0, "LA", 0), (0, "ra", 3), (0, "la", 1), (0, "la", 3),
+    (0, "RA", 0), (0, "rd", 0), (0, "RA", 1), (0, "RA", 2), (0, "LA", 2), (0, "LA", 1), (0, "ld", 1),
+    (0, "ld", 2), (0, "ld", 0), (0, "RA", 3), (0, "RD", 0), (0, "rr", 0), (0, "la", 2), (0, "rd", 1),
+    (0, "rd", 2), (0, "RR", 0), (0, "DD", (0, 0)), (1, "DD", (1, 0)), (2, "LD", 1), (2, "DD", (2, 0)),
+    (3, "DD", (1, 1)), (4, "LA", 3), (4, "ld", 3), (4, "ra", 4), (4, "LD", 2), (4, "lr", 2),
+    (4, "DD", (3, 0)), (5, "DD", (2, 1)), (6, "RD", 1), (6, "rr", 1), (6, "rd", 3), (6, "LD", 0),
+    (6, "lr", 0), (6, "ra", 5), (6, "lr", 1), (6, "RD", 2), (6, "rr", 2), (6, "DD", (0, 1)), (7, "RR", 1),
+    (13, "LD", 3), (13, "lr", 3), (14, "RD", 3), (14, "rr", 3), (14, "RA", 4), (14, "rd", 4),
+    (14, "DD", (3, 1)), (16, "RR", 2), (20, "LR", 2), (21, "RR", 3), (27, "LR", 0), (28, "RD", 4),
+    (28, "rr", 4), (29, "RA", 5), (29, "rd", 5), (32, "RR", 4), (34, "LR", 1), (39, "LR", 3), (39, "RD", 5),
+    (39, "rr", 5), (40, "DD", (0, 2)), (41, "DD", (1, 2)), (42, "DD", (2, 2)), (43, "DD", (3, 2)),
+    (46, "RR", 5),
 )
 BLOCKS = (
-    (0, 0, 0), (1, 0, 0), (2, 0, 0), (3, 0, 0), (0, 1, 0), (2, 1, 0), (0, 0, 1), (1, 0, 1), (2, 0, 1),
-    (3, 0, 1), (1, 1, 0), (0, 1, 1), (0, 0, 2), (1, 0, 2), (2, 0, 2), (3, 0, 2), (1, 1, 1), (2, 1, 1),
-    (0, 1, 2), (1, 1, 2), (2, 1, 2), (3, 1, 0), (3, 1, 1), (3, 1, 2), (0, 0, 3), (1, 0, 3), (2, 0, 3),
-    (3, 0, 3), (0, 1, 3), (1, 1, 3), (2, 1, 3), (3, 1, 3), (2, 2, 0), (2, 2, 1), (2, 2, 2), (2, 2, 3),
-    (0, 2, 0), (0, 2, 1), (0, 2, 2), (0, 2, 3), (3, 2, 0), (3, 2, 1), (0, 0, 4), (1, 0, 4), (2, 0, 4),
-    (3, 0, 4), (0, 1, 4), (1, 1, 4), (0, 0, 5), (1, 0, 5), (2, 0, 5), (3, 0, 5), (2, 1, 4), (3, 1, 4),
-    (0, 1, 5), (1, 1, 5), (2, 1, 5), (3, 1, 5), (1, 2, 0), (1, 2, 1), (1, 2, 2), (3, 2, 2), (1, 2, 3),
+    (0, 0, 0), (1, 0, 0), (2, 0, 0), (1, 1, 0), (3, 0, 0), (2, 1, 0), (0, 1, 0), (0, 0, 1), (1, 0, 1),
+    (2, 0, 1), (3, 0, 1), (0, 1, 1), (1, 1, 1), (2, 1, 1), (3, 1, 0), (3, 1, 1), (0, 0, 2), (1, 0, 2),
+    (2, 0, 2), (3, 0, 2), (0, 1, 2), (0, 0, 3), (1, 0, 3), (2, 0, 3), (3, 0, 3), (1, 1, 2), (2, 1, 2),
+    (3, 1, 2), (0, 1, 3), (1, 1, 3), (2, 1, 3), (3, 1, 3), (0, 0, 4), (1, 0, 4), (2, 0, 4), (3, 0, 4),
+    (0, 1, 4), (1, 1, 4), (2, 1, 4), (3, 1, 4), (0, 2, 0), (1, 2, 0), (2, 2, 0), (3, 2, 0), (0, 2, 1),
+    (1, 2, 1), (0, 0, 5), (1, 0, 5), (2, 0, 5), (3, 0, 5), (0, 1, 5), (1, 1, 5), (2, 1, 5), (3, 1, 5),
+    (2, 2, 1), (3, 2, 1), (0, 2, 2), (1, 2, 2), (2, 2, 2), (3, 2, 2), (0, 2, 3), (1, 2, 3), (2, 2, 3),
     (3, 2, 3), (0, 2, 4), (1, 2, 4), (2, 2, 4), (3, 2, 4), (0, 2, 5), (1, 2, 5), (2, 2, 5), (3, 2, 5),
 )
-LAG = 10
-SUMS = ((47, 47, 47, 49, 71, 75), (76, 77, 79, 81, 81, 81))
-ROUNDS = 82
+LAG = 8
+SUMS = ((45, 45, 45, 47, 55, 69), (69, 71, 75, 79, 79, 79))
+ROUNDS = 80
 
 
 def write_coded(ref, value):
     rows = value.shape[0]
     top = jnp.maximum(jnp.max(jnp.abs(value), axis=0, keepdims=True), 1e-30)
     power = jnp.ceil(jnp.log2(top))
-    coded = jnp.round(value * (jnp.exp2(-power) * TOP)).astype(jnp.int16)
+    coded = ((value * (jnp.exp2(-power) * TOP) + ROUND) - ROUND).astype(jnp.int16)
     ref[0:rows, :] = coded[:, 0:128]
     ref[rows : 2 * rows, :] = coded[:, 128:256]
     first = lax.broadcasted_iota(jnp.int32, (16, 128), 0) < 8
@@ -406,30 +408,30 @@
 
 
 def right_kernel(mask, w, rs):
-    k = pl.program_id(0)
     first = lax.axis_index("row") * 48
     tile = first // TILE
     after = jnp.minimum(tile + 1, 5)
     edge = (tile + 1) * TILE - first
     upper = lax.broadcasted_iota(jnp.int32, (48, TILE), 0) < edge
     rows = jnp.swapaxes(w[0], 0, 1)
+    low, high = mask[0, tile].astype(jnp.float32), mask[0, after].astype(jnp.float32)
     for j in range(8):
         for b in range(6):
-            kept = jnp.where(upper, mask[k, tile, j, b].astype(jnp.float32), mask[k, after, j, b].astype(jnp.float32))
+            kept = jnp.where(upper, low[j : j + 1, b : b + 1], high[j : j + 1, b : b + 1])
             rs[j // 2, j % 2 * 3 + b // 2, 0, :, b % 2 * TILE : (b % 2 + 1) * TILE] = (
                 rows[j, :, b * TILE : (b + 1) * TILE] * kept.astype(jnp.bfloat16)
             )
 
 
 def on_device(amplitudes, integrals, pair_mask, tile_mask):
-    kept = amplitudes * pair_mask[:, :, None, None].astype(jnp.bfloat16)
+    kept = jnp.where(pair_mask[:, :, None, None] != 0, amplitudes, jnp.zeros((), jnp.bfloat16))
     ls = kept.reshape(4, 4, 4, 24, 768).transpose(0, 2, 1, 3, 4).reshape(4, 4, 96, 768)
     rs = pl.pallas_call(
         right_kernel,
         grid=(4,),
         out_shape=jax.ShapeDtypeStruct((4, NS, 4, 48, NB), jnp.bfloat16),
         in_specs=[
-            pl.BlockSpec(memory_space=pltpu.SMEM),
+            pl.BlockSpec((1, 6, 8, 6), lambda k: (k, 0, 0, 0)),
             pl.BlockSpec((1, 48, 8, 768), lambda k: (k, 0, 0, 0)),
         ],
         out_specs=pl.BlockSpec((4, NS, 1, 48, NB), lambda k: (0, 0, k, 0, 0)),

time: 187 us -> 181 us (0.968); the launches traced: 184 us -> 181 us
  Pallas kernels: 180 us -> 176 us
    pallas_call x1, Pallas kernels: 170 us -> 168 us  [on_device(): pl.pallas_call(kernel, out_shape=(jax.ShapeDtypeStruct((NS, 4, 48, NB), f...]
where the time goes in v4:
time: 181 us
  Pallas kernels  176 us (97%)
  local copies, waits for them, and re-layouts  3.51 us (2%)
    pallas_call x1, Pallas kernels, on_device(): pl.pallas_call(kernel, out_shape=(jax.ShapeDtypeStruct((NS, 4, 48, NB), f...  168 us
    pallas_call x1, Pallas kernels, on_device(): pl.pallas_call(right_kernel, grid=(4,), out_shape=jax.ShapeDtypeStruct((4...  4.87 us
    pallas_call x1, Pallas kernels, on_device(): pl.pallas_call(place_kernel, grid=(2,), out_shape=jax.ShapeDtypeStruct((1...  3.83 us

profile of v4, /device:TPU:8, one launch (start us, length us, event | category | flops | bytes accessed | tf_op | source)
XLA Modules:
  0.0 180.9 jit_solution(6528649011425856038)
XLA Ops:
  0.0 0.7 broadcast_compare_fusion
  0.7 0.1 copy.5
  0.8 1.7 copy.7.mask
  2.5 0.0 copy-start
  2.5 4.9 %shard_map.46.rs = bf16[4,6,4,48,256]{4,3,2,1,0:T(8,128)(2,1)} custom-call(s32[4,6,8,6]{3,2,1,0:T(8,128)} %copy.7.mask, bf16[4,48,8,768]{3,2,1,0:T(8,128)(2,1)} %w.1), custom_call_target="tpu_custom_call" | custom-call | flops 1000000 | bytes 5000000 | tf_op jit(solution)/shard_map/pallas_call | solution.py:429
  7.4 0.0 copy-done
  7.4 0.2 broadcast_select_fusion
  7.6 1.7 copy.6
  9.3 167.8 %shard_map.47 = (f32[6,4,48,256]{3,2,1,0:T(8,128)}, s16[6,3,304,128]{3,2,1,0:T(8,128)(2,1)}, s16[6,3,112,128]{3,2,1,0:T(8,128)(2,1)}) custom-call(bf16[4,4,96,768]{3,2,1,0:T(8,128)(2,1)} %bitcast.6, bf16[4,6,4,48,256]{4,3,2,1,0:T(8,128)(2,1)} %shard_map.46.rs), custom_call_target="tpu_custom_call" | custom-call | flops 28999999488 | bytes 10000000 | tf_op jit(solution)/shard_map/pallas_call | solution.py:443
  177.1 3.8 %shard_map.48 = f32[1,4,2,192,768]{4,3,2,1,0:T(8,128)} custom-call(f32[6,4,48,256]{3,2,1,0:T(8,128)} %get-tuple-element.8.kept, s16[6,3,304,128]{3,2,1,0:T(8,128)(2,1)} %get-tuple-element.9.came0, s16[6,3,112,128]{3,2,1,0:T(8,128)(2,1)} %get-tuple-element.10.came1), custom_call_target="tpu_custom_call" | custom-call | flops 10000000 | bytes 8000000 | tf_op jit(solution)/shard_map/pallas_call | solution.py:474
Async XLA Ops:
  2.5 4.9 %copy-start = (bf16[16,4,24,768]{3,2,1,0:T(8,128)(2,1)S(1)}, bf16[16,4,24,768]{3,2,1,0:T(8,128)(2,1)}, u32[]{:S(2)}) copy-start(bf16[16,4,24,768]{3,2,1,0:T(8,128)(2,1)} %param.4) | copy-start | bytes 7077892

commit v5 on v4

--- a/solution.py
+++ b/solution.py
@@ -23,32 +23,31 @@
 
 
 EVENTS = (
-    (0, "ra", 0), (0, "ra", 1), (0, "ra", 2), (0, "LA", 0), (0, "ra", 3), (0, "la", 1), (0, "la", 3),
-    (0, "RA", 0), (0, "rd", 0), (0, "RA", 1), (0, "RA", 2), (0, "LA", 2), (0, "LA", 1), (0, "ld", 1),
-    (0, "ld", 2), (0, "ld", 0), (0, "RA", 3), (0, "RD", 0), (0, "rr", 0), (0, "la", 2), (0, "rd", 1),
-    (0, "rd", 2), (0, "RR", 0), (0, "DD", (0, 0)), (1, "DD", (1, 0)), (2, "LD", 1), (2, "DD", (2, 0)),
-    (3, "DD", (1, 1)), (4, "LA", 3), (4, "ld", 3), (4, "ra", 4), (4, "LD", 2), (4, "lr", 2),
-    (4, "DD", (3, 0)), (5, "DD", (2, 1)), (6, "RD", 1), (6, "rr", 1), (6, "rd", 3), (6, "LD", 0),
-    (6, "lr", 0), (6, "ra", 5), (6, "lr", 1), (6, "RD", 2), (6, "rr", 2), (6, "DD", (0, 1)), (7, "RR", 1),
-    (13, "LD", 3), (13, "lr", 3), (14, "RD", 3), (14, "rr", 3), (14, "RA", 4), (14, "rd", 4),
-    (14, "DD", (3, 1)), (16, "RR", 2), (20, "LR", 2), (21, "RR", 3), (27, "LR", 0), (28, "RD", 4),
-    (28, "rr", 4), (29, "RA", 5), (29, "rd", 5), (32, "RR", 4), (34, "LR", 1), (39, "LR", 3), (39, "RD", 5),
-    (39, "rr", 5), (40, "DD", (0, 2)), (41, "DD", (1, 2)), (42, "DD", (2, 2)), (43, "DD", (3, 2)),
-    (46, "RR", 5),
+    (0, "ra", 0), (0, "ra", 1), (0, "ra", 2), (0, "LA", 0), (0, "ld", 0), (0, "la", 3), (0, "la", 1),
+    (0, "RA", 0), (0, "rd", 0), (0, "LA", 1), (0, "LA", 2), (0, "ld", 2), (0, "ra", 3), (0, "ld", 1),
+    (0, "ra", 4), (0, "LD", 0), (0, "RA", 1), (0, "rd", 1), (0, "RD", 0), (0, "rr", 0), (0, "la", 2),
+    (0, "RA", 2), (0, "rd", 2), (0, "RD", 1), (0, "rr", 1), (0, "RR", 0), (0, "DD", (0, 0)),
+    (1, "DD", (1, 0)), (2, "DD", (2, 0)), (3, "LD", 2), (3, "DD", (0, 1)), (4, "RA", 3), (4, "rd", 3),
+    (4, "DD", (2, 1)), (5, "LA", 3), (5, "ld", 3), (5, "lr", 2), (5, "ra", 5), (5, "DD", (3, 0)),
+    (6, "LD", 1), (6, "lr", 1), (6, "lr", 0), (6, "RD", 2), (6, "rr", 2), (6, "RA", 4), (6, "DD", (1, 1)),
+    (7, "RR", 1), (14, "RD", 3), (14, "rr", 3), (14, "rd", 4), (14, "LD", 3), (14, "lr", 3), (14, "RR", 2),
+    (18, "DD", (3, 1)), (19, "RR", 3), (19, "LR", 2), (24, "RA", 5), (27, "RD", 4), (27, "rr", 4),
+    (27, "rd", 5), (28, "LR", 1), (31, "RR", 4), (33, "LR", 0), (38, "LR", 3), (38, "RD", 5), (38, "rr", 5),
+    (40, "DD", (0, 2)), (41, "DD", (1, 2)), (42, "DD", (2, 2)), (43, "DD", (3, 2)), (44, "RR", 5),
 )
 BLOCKS = (
-    (0, 0, 0), (1, 0, 0), (2, 0, 0), (1, 1, 0), (3, 0, 0), (2, 1, 0), (0, 1, 0), (0, 0, 1), (1, 0, 1),
-    (2, 0, 1), (3, 0, 1), (0, 1, 1), (1, 1, 1), (2, 1, 1), (3, 1, 0), (3, 1, 1), (0, 0, 2), (1, 0, 2),
-    (2, 0, 2), (3, 0, 2), (0, 1, 2), (0, 0, 3), (1, 0, 3), (2, 0, 3), (3, 0, 3), (1, 1, 2), (2, 1, 2),
-    (3, 1, 2), (0, 1, 3), (1, 1, 3), (2, 1, 3), (3, 1, 3), (0, 0, 4), (1, 0, 4), (2, 0, 4), (3, 0, 4),
-    (0, 1, 4), (1, 1, 4), (2, 1, 4), (3, 1, 4), (0, 2, 0), (1, 2, 0), (2, 2, 0), (3, 2, 0), (0, 2, 1),
-    (1, 2, 1), (0, 0, 5), (1, 0, 5), (2, 0, 5), (3, 0, 5), (0, 1, 5), (1, 1, 5), (2, 1, 5), (3, 1, 5),
+    (0, 0, 0), (1, 0, 0), (2, 0, 0), (0, 1, 0), (2, 1, 0), (3, 0, 0), (1, 1, 0), (0, 0, 1), (1, 0, 1),
+    (2, 0, 1), (3, 0, 1), (0, 1, 1), (1, 1, 1), (2, 1, 1), (0, 0, 2), (1, 0, 2), (2, 0, 2), (3, 0, 2),
+    (3, 1, 0), (0, 0, 3), (1, 0, 3), (2, 0, 3), (3, 0, 3), (3, 1, 1), (0, 1, 2), (1, 1, 2), (2, 1, 2),
+    (3, 1, 2), (0, 1, 3), (1, 1, 3), (2, 1, 3), (0, 0, 4), (1, 0, 4), (2, 0, 4), (3, 0, 4), (3, 1, 3),
+    (0, 1, 4), (1, 1, 4), (2, 1, 4), (3, 1, 4), (0, 2, 0), (1, 2, 0), (2, 2, 0), (3, 2, 0), (0, 0, 5),
+    (1, 0, 5), (2, 0, 5), (3, 0, 5), (0, 1, 5), (1, 1, 5), (2, 1, 5), (3, 1, 5), (0, 2, 1), (1, 2, 1),
     (2, 2, 1), (3, 2, 1), (0, 2, 2), (1, 2, 2), (2, 2, 2), (3, 2, 2), (0, 2, 3), (1, 2, 3), (2, 2, 3),
     (3, 2, 3), (0, 2, 4), (1, 2, 4), (2, 2, 4), (3, 2, 4), (0, 2, 5), (1, 2, 5), (2, 2, 5), (3, 2, 5),
 )
-LAG = 8
-SUMS = ((45, 45, 45, 47, 55, 69), (69, 71, 75, 79, 79, 79))
-ROUNDS = 80
+LAG = 6
+SUMS = ((43, 43, 45, 53, 57, 69), (69, 73, 77, 77, 77, 77))
+ROUNDS = 78
 
 
 def write_coded(ref, value):

time: 181 us -> 186 us (1.028)
  Pallas kernels: 176 us -> 182 us
    pallas_call x1, Pallas kernels: 168 us -> 173 us  [on_device(): pl.pallas_call(kernel, out_shape=(jax.ShapeDtypeStruct((NS, 4, 48, NB), f...]
where the time goes in v5:
time: 186 us
  Pallas kernels  182 us (98%)
  local copies, waits for them, and re-layouts  3.51 us (2%)
    pallas_call x1, Pallas kernels, on_device(): pl.pallas_call(kernel, out_shape=(jax.ShapeDtypeStruct((NS, 4, 48, NB), f...  173 us
    pallas_call x1, Pallas kernels, on_device(): pl.pallas_call(right_kernel, grid=(4,), out_shape=jax.ShapeDtypeStruct((4...  4.87 us
    pallas_call x1, Pallas kernels, on_device(): pl.pallas_call(place_kernel, grid=(2,), out_shape=jax.ShapeDtypeStruct((1...  3.83 us

profile of v5, /device:TPU:8, one launch (start us, length us, event | category | flops | bytes accessed | tf_op | source)
XLA Modules:
  0.0 186.0 jit_solution(6585285207397887169)
XLA Ops:
  0.0 0.7 broadcast_compare_fusion
  0.7 0.1 copy.5
  0.8 1.7 copy.7.mask
  2.5 0.0 copy-start
  2.5 4.9 %shard_map.46.rs = bf16[4,6,4,48,256]{4,3,2,1,0:T(8,128)(2,1)} custom-call(s32[4,6,8,6]{3,2,1,0:T(8,128)} %copy.7.mask, bf16[4,48,8,768]{3,2,1,0:T(8,128)(2,1)} %w.1), custom_call_target="tpu_custom_call" | custom-call | flops 1000000 | bytes 5000000 | tf_op jit(solution)/shard_map/pallas_call | solution.py:428
  7.4 0.0 copy-done
  7.4 0.2 broadcast_select_fusion
  7.6 1.7 copy.6
  9.3 172.9 %shard_map.47 = (f32[6,4,48,256]{3,2,1,0:T(8,128)}, s16[6,3,304,128]{3,2,1,0:T(8,128)(2,1)}, s16[6,3,112,128]{3,2,1,0:T(8,128)(2,1)}) custom-call(bf16[4,4,96,768]{3,2,1,0:T(8,128)(2,1)} %bitcast.6, bf16[4,6,4,48,256]{4,3,2,1,0:T(8,128)(2,1)} %shard_map.46.rs), custom_call_target="tpu_custom_call" | custom-call | flops 28999999488 | bytes 10000000 | tf_op jit(solution)/shard_map/pallas_call | solution.py:442
  182.2 3.8 %shard_map.48 = f32[1,4,2,192,768]{4,3,2,1,0:T(8,128)} custom-call(f32[6,4,48,256]{3,2,1,0:T(8,128)} %get-tuple-element.8.kept, s16[6,3,304,128]{3,2,1,0:T(8,128)(2,1)} %get-tuple-element.9.came0, s16[6,3,112,128]{3,2,1,0:T(8,128)(2,1)} %get-tuple-element.10.came1), custom_call_target="tpu_custom_call" | custom-call | flops 10000000 | bytes 8000000 | tf_op jit(solution)/shard_map/pallas_call | solution.py:473
Async XLA Ops:
  2.5 4.9 %copy-start = (bf16[16,4,24,768]{3,2,1,0:T(8,128)(2,1)S(1)}, bf16[16,4,24,768]{3,2,1,0:T(8,128)(2,1)}, u32[]{:S(2)}) copy-start(bf16[16,4,24,768]{3,2,1,0:T(8,128)(2,1)} %param.4) | copy-start | bytes 7077892
